TPU v7x, 32 devices: a whole 2x2x4 slice. The times are simulated.
32 devices in a mesh: wide: 4 (over y, core), narrow: 8 (over z, x).
Axes of the slice: x: 2, y: 2, z: 4, core: 2. Of those that a mesh axis runs over, the one named last changes fastest.
Arguments:
- leaf_rhs: bfloat16 [64, 1024, 256], P('wide', 'narrow'), may hold values from -6 to 6
- leaf_inv: bfloat16 [64, 256, 256], P('wide', 'narrow'), may hold values from -0.375 to 0.375
- leaf_upd: bfloat16 [64, 5, 256, 256], P('wide', None, 'narrow'), may hold values from -0.0390625 to 0.0390625
- leaf_targets: int32 [64, 5], P('wide'), may hold values from 0 to 2
- sep_rhs: bfloat16 [3, 1024, 256], P(None, 'narrow'), may hold values from -6 to 6
- sep_inv: bfloat16 [3, 256, 256], replicated, may hold values from -0.375 to 0.375
- sep_low: bfloat16 [3, 256, 256], replicated, may hold values from -0.21875 to 0.21875
Outputs:
- leaf_sol: bfloat16 [64, 1024, 256], P('wide', 'narrow')
- sep_sol: bfloat16 [3, 1024, 256], P(None, 'narrow')
All inputs are finite; a program needn't handle non-finite values.
Results may differ from a plain program's by a relative error of at most 0.012.
Values may be sent and summed in bfloat16 or wider, within the bound.
A program may use at most 64 MiB of HBM per device.

v0:
```python
import jax
import jax.numpy as jnp
from jax import lax
from jax.sharding import PartitionSpec as P


def separator_solve(gathered, sep_rhs, sep_inv, sep_low):
    nsep = sep_inv.shape[0]
    solved_list = []
    for row in range(nsep):
        reduced = sep_rhs[row].astype(jnp.float32) - gathered[row]
        for col in range(row):
            reduced = reduced - jnp.dot(
                solved_list[col],
                sep_low[row * (row - 1) // 2 + col],
                preferred_element_type=jnp.float32,
            )
        reduced = reduced.astype(jnp.bfloat16)
        solved_list.append(
            jnp.dot(reduced, sep_inv[row], preferred_element_type=jnp.float32).astype(jnp.bfloat16)
        )
    return jnp.stack(solved_list)


def body(leaf_rhs, leaf_inv, leaf_upd, leaf_targets, sep_rhs, sep_inv, sep_low):
    nsep = sep_inv.shape[0]
    nupd = leaf_upd.shape[1]
    leaves, scenarios, width = leaf_rhs.shape
    onehot = (leaf_targets[:, :, None] == jnp.arange(nsep, dtype=jnp.int32)[None, None, :]).astype(
        jnp.float32
    )
    columns = leaf_rhs
    leaf_sol = jnp.einsum(
        "lcj,lji->lci",
        columns,
        lax.all_gather(leaf_inv, "narrow", axis=1, tiled=True),
        preferred_element_type=jnp.float32,
    ).astype(jnp.bfloat16)
    start_sum = jnp.zeros((nsep, scenarios, width), jnp.float32)
    total = start_sum
    piece = lax.all_gather(leaf_upd, "narrow", axis=2, tiled=True)
    columns = leaf_sol
    for block in range(nupd):
        contrib = jnp.einsum(
            "lcj,lji->lci", columns, piece[:, block], preferred_element_type=jnp.float32
        )
        total = total + jnp.einsum("lci,ls->sci", contrib, onehot[:, block])
    gathered = total
    total = lax.psum(gathered, "wide")
    sep_sol = separator_solve(total, sep_rhs, sep_inv, sep_low)
    return (leaf_sol, sep_sol)


def solution(mesh):
    in_specs = (
        P("wide", "narrow", None),
        P("wide", "narrow", None),
        P("wide", None, "narrow", None),
        P("wide", None),
        P(None, "narrow", None),
        P(),
        P(),
    )
    out_specs = (P("wide", "narrow", None), P(None, "narrow", None))
    return jax.shard_map(body, mesh=mesh, in_specs=in_specs, out_specs=out_specs, check_vma=False)
```

profile of v0, /device:TPU:0, one launch (start us, length us, event | category | flops | bytes accessed | tf_op | source)
XLA Modules:
  0.0 266.1 jit_solution(2337355595048886722)
XLA Ops:
  7.2 0.0 copy-start
  7.2 0.0 all-gather.3.cloned.1.call-start
  7.2 0.7 all-gather.3.cloned.1.call-update
  7.9 0.0 all-gather.5.cloned.1.call-start
  8.0 0.7 all-gather.5.cloned.1.call-update
  8.7 0.0 all-reduce.2.cloned.1.call-start
  8.7 0.7 iota_compare_fusion
  9.4 52.8 %all-gather.3.cloned.1.call-done = bf16[16,256,256]{2,1,0:T(8,128)(2,1)} async-done(((bf16[16,32,256]{2,1,0:T(8,128)(2,1)}), bf16[16,256,256]{2,1,0:T(8,128)(2,1)}) %all-gather.3.cloned.1.call-update) | async-done | bytes 2097168 | tf_op jit(solution)/shard_map/all_gather | solution.py:36
  62.2 2.0 convolution_convert_fusion
  64.2 0.0 copy-start.1
  64.3 149.5 %all-gather.5.cloned.1.call-done = bf16[16,5,256,256]{3,2,1,0:T(8,128)(2,1)} async-done(((bf16[16,5,32,256]{3,2,1,0:T(8,128)(2,1)}), bf16[16,5,256,256]{3,2,1,0:T(8,128)(2,1)}) %all-gather.5.cloned.1.call-update) | async-done | bytes 10485776 | tf_op jit(solution)/shard_map/all_gather | solution.py:41
  213.8 2.2 fusion.3
  216.0 0.7 fusion.11
  216.6 2.7 %fusion.1 = bf16[16,128,256]{2,1,0:T(8,128)(2,1)S(1)} fusion(bf16[16,128,256]{2,1,0:T(8,128)(2,1)S(1)} %convolution_convert_fusion, bf16[16,5,256,256]{3,2,1,0:T(8,128)(2,1)} %all-gather.5.cloned.1.call-done), kind=kOutput, calls=%fused_computation.3 | convolution fusion | flops 268435456 | bytes 4194304 | tf_op jit(solution)/shard_map/lcj,lji->lci/dot_general | solution.py:44
  219.4 0.7 fusion.7
  220.1 0.5 fusion.2
  220.5 0.7 fusion.9
  221.2 0.5 fusion.4
  221.7 0.8 fusion.21
  222.4 0.5 fusion
  222.9 0.0 copy-start.5
  222.9 0.0 copy-start.4
  222.9 0.0 copy-start.3
  222.9 1.5 fusion.24
  224.4 0.0 all-reduce.2.cloned.1.call-update
  224.5 31.5 %all-reduce.2.cloned.1.call-done = f32[3,128,256]{2,0,1:T(4,128)} async-done(((f32[3,128,256]{2,0,1:T(4,128)}), f32[3,128,256]{2,0,1:T(4,128)}) %all-reduce.2.cloned.1.call-update) | async-done | bytes 393232 | tf_op jit(solution)/shard_map/psum | solution.py:49
  256.0 1.9 slice_subtract_fusion.1
  257.9 0.2 convolution_convert_fusion.3
  258.1 0.3 convolution_convert_fusion.2
  258.4 0.2 convolution_subtract_fusion.1
  258.6 0.3 fusion.29
  258.9 0.7 pad_maximum_fusion
  (8 shorter events, 0.0 us)
Async XLA Ops:
  7.2 55.0 %copy-start = (bf16[16,128,256]{2,1,0:T(8,128)(2,1)S(1)}, bf16[16,128,256]{2,1,0:T(8,128)(2,1)}, u32[]{:S(2)}) copy-start(bf16[16,128,256]{2,1,0:T(8,128)(2,1)} %param.7) | copy-start | bytes 3145732
  7.2 55.0 %all-gather.3.cloned.1.call-start = ((), (), s32[]{:S(2)}) async-start(), calls=%async_computation | async-start | bytes 2359296 | tf_op jit(solution)/shard_map/all_gather | solution.py:36
  7.9 205.8 %all-gather.5.cloned.1.call-start = ((), (), s32[]{:S(2)}) async-start(), calls=%async_computation.1 | async-start | bytes 11796480 | tf_op jit(solution)/shard_map/all_gather | solution.py:41
  8.7 247.4 %all-reduce.2.cloned.1.call-start = ((), (), s32[]{:S(2)}) async-start(), calls=%async_computation.2 | async-start | bytes 1048576 | tf_op jit(solution)/shard_map/psum | solution.py:49
  64.2 158.2 %copy-start.1 = (bf16[16,128,256]{2,1,0:T(8,128)(2,1)}, bf16[16,128,256]{2,1,0:T(8,128)(2,1)S(1)}, u32[]{:S(2)}) copy-start(bf16[16,128,256]{2,1,0:T(8,128)(2,1)S(1)} %convolution_convert_fusion) | copy-start | bytes 3145732
  213.8 6.3 %copy-start.2 = (bf16[16,5,256,256]{3,2,1,0:T(8,128)(2,1)S(1)}, bf16[16,5,256,256]{3,2,1,0:T(8,128)(2,1)}, u32[]{:S(2)}) copy-start(bf16[16,5,256,256]{3,2,1,0:T(8,128)(2,1)} %all-gather.5.cloned.1.call-done) | copy-start | bytes 31457284
  222.9 1.6 copy-start.5
  222.9 35.0 %copy-start.4 = (bf16[3,256,256]{2,1,0:T(8,128)(2,1)S(1)}, bf16[3,256,256]{2,1,0:T(8,128)(2,1)}, u32[]{:S(2)}) copy-start(bf16[3,256,256]{2,1,0:T(8,128)(2,1)} %param.12) | copy-start | bytes 1179652
  222.9 35.2 %copy-start.3 = (bf16[3,256,256]{2,1,0:T(8,128)(2,1)S(1)}, bf16[3,256,256]{2,1,0:T(8,128)(2,1)}, u32[]{:S(2)}) copy-start(bf16[3,256,256]{2,1,0:T(8,128)(2,1)} %param.13) | copy-start | bytes 1179652
Sparse Core Ops, SparseCore 0:
  10.2 51.9 all-gather.2
  64.4 149.3 all-gather.4
  224.6 31.4 all-reduce.1
where the time goes:
time: 266 us
  waiting for transfers between devices  235 us (88%)
  between operations  13.9 us (5%)
  matrix products  13.5 us (5%)
  other arithmetic  3.29 us (1%)
    all_gather x1, waiting for transfers between devices, body(): piece = lax.all_gather(leaf_upd, 'narrow', axis=2, tiled=True)  150 us
    all_gather x1, waiting for transfers between devices, body(): lax.all_gather(leaf_inv, 'narrow', axis=1, tiled=True)  52.8 us
    psum x1, waiting for transfers between devices, body(): total = lax.psum(gathered, 'wide')  31.5 us
    dot_general x5, matrix products, body(): jnp.einsum('lcj,lji->lci', columns, piece[:, block], preferred_element_ty...  6.28 us
  transfers between devices with their start and end apart: 3, of which 3 were waited for; matrix products, arithmetic and copies ran while one was open for 1% of the time, Pallas kernels for 0%

commit v1 on v0

--- a/solution.py
+++ b/solution.py
@@ -2,6 +2,22 @@
 import jax.numpy as jnp
 from jax import lax
 from jax.sharding import PartitionSpec as P
+
+
+def ring_product(x, axis, dim, product):
+    count, position, rows = (lax.axis_size(axis), lax.axis_index(axis), x.shape[dim])
+    ahead = [(i, (i + 1) % count) for i in range(count)]
+    left = [(i, (i - 1) % count) for i in range(count)]
+    halfway = count // 2
+    from_left = from_right = x
+    total = product(x, position * rows)
+    for lap in range(1, halfway + 1):
+        from_left = lax.ppermute(from_left, axis, ahead)
+        if lap < count - halfway:
+            from_right = lax.ppermute(from_right, axis, left)
+            total = total + product(from_right, (position + lap) % count * rows)
+        total = total + product(from_left, (position - lap) % count * rows)
+    return total
 
 
 def separator_solve(gathered, sep_rhs, sep_inv, sep_low):
@@ -30,11 +46,16 @@
         jnp.float32
     )
     columns = leaf_rhs
-    leaf_sol = jnp.einsum(
-        "lcj,lji->lci",
-        columns,
-        lax.all_gather(leaf_inv, "narrow", axis=1, tiled=True),
-        preferred_element_type=jnp.float32,
+    leaf_sol = ring_product(
+        leaf_inv,
+        "narrow",
+        1,
+        lambda own_block, offset: jnp.einsum(
+            "lcj,lji->lci",
+            lax.dynamic_slice_in_dim(columns, offset, own_block.shape[1], axis=2),
+            own_block,
+            preferred_element_type=jnp.float32,
+        ),
     ).astype(jnp.bfloat16)
     start_sum = jnp.zeros((nsep, scenarios, width), jnp.float32)
     total = start_sum

time: 266 us -> 235 us (0.88)
  waiting for transfers between devices: 235 us -> 180 us
  starting transfers between devices: 0.11 us -> 19.8 us
  matrix products: 13.5 us -> 16.8 us
    all_gather x1 -> x0, waiting for transfers between devices: 52.8 us -> none  [body(): lax.all_gather(leaf_inv, 'narrow', axis=1, tiled=True)]
    all_gather x1, waiting for transfers between devices: 150 us -> 104 us  [body(): piece = lax.all_gather(leaf_upd, 'narrow', axis=2, tiled=True)]
    ppermute x0 -> x7, waiting for transfers between devices: none -> 44.5 us  [the longest x4 28.1 us: ring_product(): from_left = lax.ppermute(from_left, axis, ahead)]
    ppermute x0 -> x7, starting transfers between devices: none -> 19.8 us  [the longest x3 15.7 us: ring_product(): from_right = lax.ppermute(from_right, axis, left)]
    dot_general x1 -> x8, matrix products: 2.03 us -> 5.33 us  [body(): jnp.einsum('lcj,lji->lci', lax.dynamic_slice_in_dim(columns, offset, own_...]
  transfers between devices with their start and end apart: 3 -> 9, of which waited for: 3 -> 6; matrix products, arithmetic and copies ran while one was open for 1% -> 3% of each run, Pallas kernels for 0% -> 0%
where the time goes in v1:
time: 235 us
  waiting for transfers between devices  180 us (77%)
  starting transfers between devices  19.8 us (8%)
  matrix products  16.8 us (7%)
  between operations  14.3 us (6%)
  other arithmetic  3.37 us (1%)
    all_gather x1, waiting for transfers between devices, body(): piece = lax.all_gather(leaf_upd, 'narrow', axis=2, tiled=True)  104 us
    psum x1, waiting for transfers between devices, body(): total = lax.psum(gathered, 'wide')  31.5 us
    ppermute x4, waiting for transfers between devices, ring_product(): from_left = lax.ppermute(from_left, axis, ahead)  28.1 us
    ppermute x3, waiting for transfers between devices, ring_product(): from_right = lax.ppermute(from_right, axis, left)  16.4 us
    ppermute x3, starting transfers between devices, ring_product(): from_right = lax.ppermute(from_right, axis, left)  15.7 us
    dot_general x5, matrix products, body(): jnp.einsum('lcj,lji->lci', columns, piece[:, block], preferred_element_ty...  6.28 us
    dot_general x8, matrix products, body(): jnp.einsum('lcj,lji->lci', lax.dynamic_slice_in_dim(columns, offset, own_...  5.33 us
  transfers between devices with their start and end apart: 9, of which 6 were waited for; matrix products, arithmetic and copies ran while one was open for 3% of the time, Pallas kernels for 0%

profile of v1, /device:TPU:0, one launch (start us, length us, event | category | flops | bytes accessed | tf_op | source)
XLA Modules:
  0.0 234.6 jit_solution(15314931950209694072)
XLA Ops:
  7.2 0.7 all-gather.2.cloned.1.call-update
  8.0 6.0 %collective-permute-start = (bf16[16,32,256]{2,1,0:T(8,128)(2,1)}, bf16[16,32,256]{2,1,0:T(8,128)(2,1)S(1)}, u32[]{:S(2)}, u32[]{:S(2)}) collective-permute-start(bf16[16,32,256]{2,1,0:T(8,128)(2,1)} %param.8), channel_id=1, source_target_pairs={{0,7},{1,0},{2,1},{3,2},{4,3},{5,4},{6,5},{7,6},{8,15},{9,8},{10,9... | collective-permute-start | bytes 786440 | tf_op jit(solution)/shard_map/ppermute | solution.py:17
  14.0 0.7 iota_compare_fusion
  14.7 1.5 fusion.43
  16.1 3.7 %collective-permute-done = bf16[16,32,256]{2,1,0:T(8,128)(2,1)S(1)} collective-permute-done((bf16[16,32,256]{2,1,0:T(8,128)(2,1)}, bf16[16,32,256]{2,1,0:T(8,128)(2,1)S(1)}, u32[]{:S(2)}, u32[]{:S(2)}) %collective-permute-start) | collective-permute-done | bytes 262176 | tf_op jit(solution)/shard_map/ppermute | solution.py:17
  19.9 6.2 %collective-permute-start.2 = (bf16[16,32,256]{2,1,0:T(8,128)(2,1)S(1)}, bf16[16,32,256]{2,1,0:T(8,128)(2,1)S(1)}, u32[]{:S(2)}, u32[]{:S(2)}) collective-permute-start(bf16[16,32,256]{2,1,0:T(8,128)(2,1)S(1)} %collective-permute-done), channel_id=1, source_target_pairs={{0,7},{1,0},{2,1},{3,2},{4,3},{5,4},{6,5},{7,6},{8,15},{9,8},{10,9... | collective-permute-start | bytes 786440 | tf_op jit(solution)/shard_map/ppermute | solution.py:17
  26.0 1.2 collective-permute-start.3
  27.2 0.5 fusion.39
  27.7 0.5 fusion.41
  28.2 12.7 %collective-permute-done.2 = bf16[16,32,256]{2,1,0:T(8,128)(2,1)S(1)} collective-permute-done((bf16[16,32,256]{2,1,0:T(8,128)(2,1)S(1)}, bf16[16,32,256]{2,1,0:T(8,128)(2,1)S(1)}, u32[]{:S(2)}, u32[]{:S(2)}) %collective-permute-start.2) | collective-permute-done | bytes 262176 | tf_op jit(solution)/shard_map/ppermute | solution.py:17
  40.9 3.5 %collective-permute-start.4 = (bf16[16,32,256]{2,1,0:T(8,128)(2,1)S(1)}, bf16[16,32,256]{2,1,0:T(8,128)(2,1)S(1)}, u32[]{:S(2)}, u32[]{:S(2)}) collective-permute-start(bf16[16,32,256]{2,1,0:T(8,128)(2,1)S(1)} %collective-permute-done.2), channel_id=1, source_target_pairs={{0,7},{1,0},{2,1},{3,2},{4,3},{5,4},{6,5},{7,6},{8,15},{9,8},{10,9... | collective-permute-start | bytes 786440 | tf_op jit(solution)/shard_map/ppermute | solution.py:17
  44.4 1.4 collective-permute-start.5
  45.8 0.5 fusion.35
  46.3 0.5 fusion.37
  46.8 14.0 %collective-permute-done.5 = bf16[16,32,256]{2,1,0:T(8,128)(2,1)S(1)} collective-permute-done((bf16[16,32,256]{2,1,0:T(8,128)(2,1)S(1)}, bf16[16,32,256]{2,1,0:T(8,128)(2,1)S(1)}, u32[]{:S(2)}, u32[]{:S(2)}) %collective-permute-start.5) | collective-permute-done | bytes 262176 | tf_op jit(solution)/shard_map/ppermute | solution.py:15
  60.8 1.5 collective-permute-start.6
  62.2 0.5 fusion.31
  62.7 0.5 fusion.33
  63.2 14.1 %collective-permute-done.6 = bf16[16,32,256]{2,1,0:T(8,128)(2,1)S(1)} collective-permute-done((bf16[16,32,256]{2,1,0:T(8,128)(2,1)S(1)}, bf16[16,32,256]{2,1,0:T(8,128)(2,1)S(1)}, u32[]{:S(2)}, u32[]{:S(2)}) %collective-permute-start.6) | collective-permute-done | bytes 262176 | tf_op jit(solution)/shard_map/ppermute | solution.py:15
  77.4 0.9 add_convert_fusion
  78.3 103.6 %all-gather.2.cloned.1.call-done = bf16[16,5,256,256]{3,2,1,0:T(8,128)(2,1)} async-done(((bf16[16,5,32,256]{3,2,1,0:T(8,128)(2,1)}), bf16[16,5,256,256]{3,2,1,0:T(8,128)(2,1)}) %all-gather.2.cloned.1.call-update) | async-done | bytes 10485776 | tf_op jit(solution)/shard_map/all_gather | solution.py:62
  181.9 2.2 fusion.3
  184.1 0.7 fusion.11
  184.8 2.7 %fusion.1 = bf16[16,128,256]{2,1,0:T(8,128)(2,1)S(1)} fusion(bf16[16,128,256]{2,1,0:T(8,128)(2,1)S(1)} %add_convert_fusion, bf16[16,5,256,256]{3,2,1,0:T(8,128)(2,1)} %all-gather.2.cloned.1.call-done), kind=kOutput, calls=%fused_computation.3 | convolution fusion | flops 268435456 | bytes 4194304 | tf_op jit(solution)/shard_map/lcj,lji->lci/dot_general | solution.py:65
  187.5 0.7 fusion.7
  188.7 0.7 fusion.9
  189.3 0.5 fusion.4
  189.8 0.8 fusion.21
  191.1 1.5 fusion.24
  192.6 31.5 %all-reduce.2.cloned.1.call-done = f32[3,128,256]{2,0,1:T(4,128)} async-done(((f32[3,128,256]{2,0,1:T(4,128)}), f32[3,128,256]{2,0,1:T(4,128)}) %all-reduce.2.cloned.1.call-update) | async-done | bytes 393232 | tf_op jit(solution)/shard_map/psum | solution.py:70
  224.1 2.0 slice_subtract_fusion.1
  227.1 0.7 pad_maximum_fusion
  (26 shorter events, 2.0 us)
Async XLA Ops:
  7.2 7.5 %copy-start = (bf16[16,128,256]{2,1,0:T(8,128)(2,1)S(1)}, bf16[16,128,256]{2,1,0:T(8,128)(2,1)}, u32[]{:S(2)}) copy-start(bf16[16,128,256]{2,1,0:T(8,128)(2,1)} %param.7) | copy-start | bytes 3145732
  7.2 174.7 %all-gather.2.cloned.1.call-start = ((), (), s32[]{:S(2)}) async-start(), calls=%async_computation | async-start | bytes 11796480 | tf_op jit(solution)/shard_map/all_gather | solution.py:62
  7.9 216.2 %all-reduce.2.cloned.1.call-start = ((), (), s32[]{:S(2)}) async-start(), calls=%async_computation.1 | async-start | bytes 1048576 | tf_op jit(solution)/shard_map/psum | solution.py:70
  8.0 11.9 %collective-permute-start = (bf16[16,32,256]{2,1,0:T(8,128)(2,1)}, bf16[16,32,256]{2,1,0:T(8,128)(2,1)S(1)}, u32[]{:S(2)}, u32[]{:S(2)}) collective-permute-start(bf16[16,32,256]{2,1,0:T(8,128)(2,1)} %param.8), channel_id=1, source_target_pairs={{0,7},{1,0},{2,1},{3,2},{4,3},{5,4},{6,5},{7,6},{8,15},{9,8},{10,9... | collective-permute-start | bytes 786440 | tf_op jit(solution)/shard_map/ppermute | solution.py:17
  14.0 12.0 %collective-permute-start.1 = (bf16[16,32,256]{2,1,0:T(8,128)(2,1)}, bf16[16,32,256]{2,1,0:T(8,128)(2,1)S(1)}, u32[]{:S(2)}, u32[]{:S(2)}) collective-permute-start(bf16[16,32,256]{2,1,0:T(8,128)(2,1)} %param.8), channel_id=1, source_target_pairs={{0,1},{1,2},{2,3},{3,4},{4,5},{5,6},{6,7},{7,0},{8,9},{9,10},{10,1... | collective-permute-start | bytes 786440 | tf_op jit(solution)/shard_map/ppermute | solution.py:15
  19.9 21.0 %collective-permute-start.2 = (bf16[16,32,256]{2,1,0:T(8,128)(2,1)S(1)}, bf16[16,32,256]{2,1,0:T(8,128)(2,1)S(1)}, u32[]{:S(2)}, u32[]{:S(2)}) collective-permute-start(bf16[16,32,256]{2,1,0:T(8,128)(2,1)S(1)} %collective-permute-done), channel_id=1, source_target_pairs={{0,7},{1,0},{2,1},{3,2},{4,3},{5,4},{6,5},{7,6},{8,15},{9,8},{10,9... | collective-permute-start | bytes 786440 | tf_op jit(solution)/shard_map/ppermute | solution.py:17
  26.0 18.4 %collective-permute-start.3 = (bf16[16,32,256]{2,1,0:T(8,128)(2,1)S(1)}, bf16[16,32,256]{2,1,0:T(8,128)(2,1)S(1)}, u32[]{:S(2)}, u32[]{:S(2)}) collective-permute-start(bf16[16,32,256]{2,1,0:T(8,128)(2,1)S(1)} %collective-permute-done.1), channel_id=1, source_target_pairs={{0,1},{1,2},{2,3},{3,4},{4,5},{5,6},{6,7},{7,0},{8,9},{9,10},{10,1... | collective-permute-start | bytes 786440 | tf_op jit(solution)/shard_map/ppermute | solution.py:15
  40.9 21.8 %collective-permute-start.4 = (bf16[16,32,256]{2,1,0:T(8,128)(2,1)S(1)}, bf16[16,32,256]{2,1,0:T(8,128)(2,1)S(1)}, u32[]{:S(2)}, u32[]{:S(2)}) collective-permute-start(bf16[16,32,256]{2,1,0:T(8,128)(2,1)S(1)} %collective-permute-done.2), channel_id=1, source_target_pairs={{0,7},{1,0},{2,1},{3,2},{4,3},{5,4},{6,5},{7,6},{8,15},{9,8},{10,9... | collective-permute-start | bytes 786440 | tf_op jit(solution)/shard_map/ppermute | solution.py:17
  44.4 16.3 %collective-permute-start.5 = (bf16[16,32,256]{2,1,0:T(8,128)(2,1)S(1)}, bf16[16,32,256]{2,1,0:T(8,128)(2,1)S(1)}, u32[]{:S(2)}, u32[]{:S(2)}) collective-permute-start(bf16[16,32,256]{2,1,0:T(8,128)(2,1)S(1)} %collective-permute-done.3), channel_id=1, source_target_pairs={{0,1},{1,2},{2,3},{3,4},{4,5},{5,6},{6,7},{7,0},{8,9},{9,10},{10,1... | collective-permute-start | bytes 786440 | tf_op jit(solution)/shard_map/ppermute | solution.py:15
  60.8 16.6 %collective-permute-start.6 = (bf16[16,32,256]{2,1,0:T(8,128)(2,1)S(1)}, bf16[16,32,256]{2,1,0:T(8,128)(2,1)S(1)}, u32[]{:S(2)}, u32[]{:S(2)}) collective-permute-start(bf16[16,32,256]{2,1,0:T(8,128)(2,1)S(1)} %collective-permute-done.5), channel_id=1, source_target_pairs={{0,1},{1,2},{2,3},{3,4},{4,5},{5,6},{6,7},{7,0},{8,9},{9,10},{10,1... | collective-permute-start | bytes 786440 | tf_op jit(solution)/shard_map/ppermute | solution.py:15
  78.3 112.3 %copy-start.1 = (bf16[16,128,256]{2,1,0:T(8,128)(2,1)}, bf16[16,128,256]{2,1,0:T(8,128)(2,1)S(1)}, u32[]{:S(2)}) copy-start(bf16[16,128,256]{2,1,0:T(8,128)(2,1)S(1)} %add_convert_fusion) | copy-start | bytes 3145732
  181.9 6.3 %copy-start.2 = (bf16[16,5,256,256]{3,2,1,0:T(8,128)(2,1)S(1)}, bf16[16,5,256,256]{3,2,1,0:T(8,128)(2,1)}, u32[]{:S(2)}) copy-start(bf16[16,5,256,256]{3,2,1,0:T(8,128)(2,1)} %all-gather.2.cloned.1.call-done) | copy-start | bytes 31457284
  191.0 1.6 copy-start.5
  191.0 35.1 %copy-start.4 = (bf16[3,256,256]{2,1,0:T(8,128)(2,1)S(1)}, bf16[3,256,256]{2,1,0:T(8,128)(2,1)}, u32[]{:S(2)}) copy-start(bf16[3,256,256]{2,1,0:T(8,128)(2,1)} %param.12) | copy-start | bytes 1179652
  191.0 35.2 %copy-start.3 = (bf16[3,256,256]{2,1,0:T(8,128)(2,1)S(1)}, bf16[3,256,256]{2,1,0:T(8,128)(2,1)}, u32[]{:S(2)}) copy-start(bf16[3,256,256]{2,1,0:T(8,128)(2,1)} %param.13) | copy-start | bytes 1179652
Sparse Core Ops, SparseCore 0:
  10.2 171.6 all-gather.1
  192.7 31.3 all-reduce.1
